TPU v7x, 128 devices: a whole 4x4x4 slice. The times are simulated.
128 devices in a mesh: dp: 32 (over x, y, core), fsdp: 4 (over z).
Axes of the slice: x: 4, y: 4, z: 4, core: 2. Of those that a mesh axis runs over, the one named last changes fastest.
Arguments:
- tokens: bfloat16 [65536, 4608], P(('dp', 'fsdp')), as said below
- rmsnorm_gain_vector: bfloat16 [4608], replicated, may hold values from 0.099609375 to 1.8984375
- tied_query_matrix: bfloat16 [4608, 2048], P('fsdp'), may hold values from -0.09375 to 0.09375
- adapter_down_matrix: bfloat16 [4608, 128], P('fsdp'), may hold values from -0.09375 to 0.09375
- adapter_up_matrix: bfloat16 [128, 2048], replicated, may hold values from -0.5 to 0.5
- depth: int32 [4096], P(('dp', 'fsdp')), may hold values from 1 to 3, as said below
- destination: int32 [4096], P(('dp', 'fsdp')), may hold values from 0 to 31, as said below
- cotangent: bfloat16 [32768, 2048], P(('dp', 'fsdp')), may hold values from -6 to 6
Outputs:
- query: bfloat16 [32768, 2048], P(('dp', 'fsdp'))
- grad_tokens: bfloat16 [65536, 4608], P(('dp', 'fsdp'))
- grad_down: float32 [4608, 128], replicated
- grad_up: float32 [128, 2048], replicated
Inputs may be any that keep to these rules, and one draw needn't show every extreme that they name: Blocks that stop before this recursion have depth 1; the others have depth 2 or 3. `destination`: only entries of surviving blocks are read. Each dp index is named by exactly 16 surviving blocks with its own fsdp index, and by at most 1 surviving blocks of any one device; both bounds are reached in every draw. `tokens`: float values of mixed row and feature scales.
All inputs are finite; a program needn't handle non-finite values.
Results may differ from a plain program's by a relative error of at most 0.0053.
Values may be sent and summed in bfloat16 or wider, within the bound.
No kernel may reach another device: no remote copies, remote signals or barrier semaphores. Data moves between devices by JAX's collectives and lax.ppermute only.
A program may use at most 128 MiB of HBM per device.

v0:
```python
import jax
import jax.numpy as jnp
from jax import lax
from jax.sharding import PartitionSpec as P


def arrange(live, target, dp_count, slot_count):
    blocks = live.shape[0]
    order = jnp.arange(blocks, dtype=jnp.int32)
    same = (target[:, None] == target[None, :]) & live[None, :] & (order[None, :] < order[:, None])
    within = jnp.sum(same.astype(jnp.int32), axis=1)
    slot_of = target * slot_count + within
    places = jnp.arange(dp_count * slot_count, dtype=jnp.int32)
    hits = live[None, :] & (slot_of[None, :] == places[:, None])
    source = jnp.sum(jnp.where(hits, order[None, :], 0), axis=1)
    filled = jnp.any(hits, axis=1)
    return (slot_of, source, filled)


def compact(flags, capacity):
    count = flags.shape[0]
    rank = jnp.cumsum(flags.astype(jnp.int32)) - 1
    wanted = jnp.arange(capacity, dtype=jnp.int32)
    places = jnp.arange(count, dtype=jnp.int32)
    match = flags[None, :] & (rank[None, :] == wanted[:, None])
    pick = jnp.sum(jnp.where(match, places[None, :], 0), axis=1)
    return (pick, jnp.clip(rank, 0, capacity - 1))


def project_surviving(
    input_rows,
    incoming_gradient_rows,
    rmsnorm_gain_vector,
    tied_query_matrix,
    adapter_down_matrix,
    adapter_up_matrix,
):
    xfloat = input_rows.astype(jnp.float32)
    inverse = lax.rsqrt(jnp.mean(xfloat * xfloat, axis=-1, keepdims=True) + 1e-06)
    normed = xfloat * inverse
    gain_f = rmsnorm_gain_vector.astype(jnp.float32)
    normalized_blocks = (normed * gain_f).astype(jnp.bfloat16)
    full_weight, full_down = (
        lax.all_gather(tied_query_matrix, "fsdp", axis=0, tiled=True),
        lax.all_gather(adapter_down_matrix, "fsdp", axis=0, tiled=True),
    )
    shared_output = jnp.dot(normalized_blocks, full_weight, preferred_element_type=jnp.float32)
    lowrank_hidden = jnp.dot(
        normalized_blocks, full_down, preferred_element_type=jnp.float32
    ).astype(jnp.bfloat16)
    projected_query_rows = (
        shared_output
        + jnp.dot(lowrank_hidden, adapter_up_matrix, preferred_element_type=jnp.float32)
    ).astype(jnp.bfloat16)
    gradient_lowrank = jnp.einsum(
        "da,va->dv", incoming_gradient_rows, adapter_up_matrix, preferred_element_type=jnp.float32
    ).astype(jnp.bfloat16)
    gradient_normalized = jnp.einsum(
        "rq,dq->rd", incoming_gradient_rows, full_weight, preferred_element_type=jnp.float32
    )
    gradient_normalized = gradient_normalized + jnp.einsum(
        "rk,dk->rd", gradient_lowrank, full_down, preferred_element_type=jnp.float32
    )
    grad_up = jnp.einsum(
        "rk,rq->kq", lowrank_hidden, incoming_gradient_rows, preferred_element_type=jnp.float32
    )
    grad_down = jnp.einsum(
        "rd,rk->dk", normalized_blocks, gradient_lowrank, preferred_element_type=jnp.float32
    )
    dscaled = gradient_normalized * gain_f
    grad_rows = inverse * (dscaled - normed * jnp.mean(dscaled * normed, axis=-1, keepdims=True))
    return (projected_query_rows, grad_rows.astype(jnp.bfloat16), grad_down, grad_up)


def body(
    tokens,
    rmsnorm_gain_vector,
    tied_query_matrix,
    adapter_down_matrix,
    adapter_up_matrix,
    depth,
    destination,
    cotangent,
):
    dp_count = lax.axis_size("dp")
    blocks = depth.shape[0]
    block_rows = tokens.shape[0] // blocks
    width = tokens.shape[1]
    capacity = cotangent.shape[0] // block_rows
    slot_count = max(1, blocks // dp_count)
    live = depth >= 2
    slot_of, source, filled = arrange(live, destination, dp_count, slot_count)
    flag_send = filled.astype(jnp.bfloat16).reshape(dp_count, slot_count)
    zero_b = jnp.zeros((), jnp.bfloat16)
    token_blocks = tokens.reshape(blocks, block_rows, width)
    send_rows = jnp.where(filled[:, None, None], jnp.take(token_blocks, source, axis=0), zero_b)
    send_rows = send_rows.reshape(dp_count, slot_count, block_rows, width)
    got_rows, got_flags = (
        lax.all_to_all(send_rows, "dp", split_axis=0, concat_axis=0, tiled=True),
        lax.all_to_all(flag_send, "dp", split_axis=0, concat_axis=0, tiled=True),
    )
    flags = got_flags.reshape(-1) > 0.5
    pick, rank = compact(flags, capacity)
    input_rows = jnp.take(got_rows.reshape(dp_count * slot_count, block_rows, width), pick, axis=0)
    query, grad_rows, grad_down, grad_up = project_surviving(
        input_rows.reshape(capacity * block_rows, width),
        cotangent,
        rmsnorm_gain_vector,
        tied_query_matrix,
        adapter_down_matrix,
        adapter_up_matrix,
    )
    back = jnp.take(grad_rows.reshape(capacity, block_rows, width), rank, axis=0)
    back = jnp.where(flags[:, None, None], back, zero_b).reshape(
        dp_count, slot_count, block_rows, width
    )
    returned = lax.all_to_all(back, "dp", split_axis=0, concat_axis=0, tiled=True)
    grad_blocks = jnp.take(
        returned.reshape(dp_count * slot_count, block_rows, width), slot_of, axis=0
    )
    grad_tokens = jnp.where(live[:, None, None], grad_blocks, zero_b).reshape(
        tokens.shape[0], width
    )
    grad_down, grad_up = lax.psum((grad_down, grad_up), ("dp", "fsdp"))
    return (query, grad_tokens, grad_down, grad_up)


def solution(mesh):
    in_specs = (
        P(("dp", "fsdp"), None),
        P(),
        P("fsdp", None),
        P("fsdp", None),
        P(),
        P(("dp", "fsdp")),
        P(("dp", "fsdp")),
        P(("dp", "fsdp"), None),
    )
    out_specs = (P(("dp", "fsdp"), None), P(("dp", "fsdp"), None), P(), P())
    return jax.shard_map(body, mesh=mesh, in_specs=in_specs, out_specs=out_specs, check_vma=False)
```

profile of v0, /device:TPU:1, one launch (start us, length us, event | category | flops | bytes accessed | tf_op | source)
XLA Modules:
  0.0 448.2 jit_solution(3391662864419010734)
XLA Ops:
  7.2 0.0 copy-start
  7.2 0.0 all-gather.5.cloned.1.call-start
  7.2 0.7 all-gather.5.cloned.1.call-update
  7.9 0.0 all-gather.3.cloned.1.call-start
  8.0 0.7 all-gather.3.cloned.1.call-update
  8.7 0.2 convert_reduce_fusion
  8.9 0.1 fusion.7
  9.0 0.7 copy.18
  9.8 8.6 %all-to-all-start = ((bf16[32,1,1]{2,1,0:T(2,128)(2,1)}), bf16[32,1,1]{2,1,0:T(2,128)(2,1)S(1)}, u32[]{:S(2)}, u32[]{:S(2)}) async-start(bf16[32,1,1]{2,1,0:T(2,128)(2,1)} %copy.18), calls=%async_computation | async-start | bytes 32768 | tf_op jit(solution)/shard_map/all_to_all | solution.py:100
  18.4 0.1 select_reduce_fusion
  18.5 5.4 %gather_fusion.2 = bf16[32,16,4608]{2,1,0:T(8,128)(2,1)} fusion(bf16[32,16,4608]{2,1,0:T(8,128)(2,1)} %bitcast.43, s32[1024]{0:T(1024)S(1)} %pad_clamp_fusion.3), kind=kCustom, calls=%fused_computation.clone | custom fusion | bytes 9437312 | tf_op jit(solution)/shard_map/jit(_take)/gather | solution.py:96
  23.9 5.1 %fusion.2 = bf16[32,1,16,4608]{3,2,1,0:T(8,128)(2,1)} fusion(bf16[32,16,4608]{2,1,0:T(8,128)(2,1)} %gather_fusion.2, pred[32]{0:T(512)(128)(4,1)S(1)} %compare_and_fusion.1, pred[32]{0:T(512)(128)(4,1)S(1)} %fusion.7), kind=kLoop, calls=%fused_computation.10 | loop fusion | flops 4718592 | bytes 9437248 | tf_op jit(solution)/shard_map/reshape | solution.py:97
  29.0 0.0 all-to-all-done
  29.0 7.6 %all-to-all-start.1 = ((bf16[32,1,16,4608]{3,2,1,0:T(8,128)(2,1)}), bf16[32,1,16,4608]{3,2,1,0:T(8,128)(2,1)}, u32[]{:S(2)}, u32[]{:S(2)}) async-start(bf16[32,1,16,4608]{3,2,1,0:T(8,128)(2,1)} %fusion.2), calls=%async_computation.1 | async-start | bytes 9437184 | tf_op jit(solution)/shard_map/all_to_all | solution.py:99
  36.6 0.0 copy-done.4
  36.6 0.4 convolution_convert_fusion
  37.1 0.7 compare_reduce_fusion
  37.7 0.1 reduce-window.4
  37.8 0.1 fusion.4
  37.9 0.1 select_reduce_fusion.1
  38.0 0.1 broadcast_in_dim.107
  38.1 0.1 broadcast_in_dim.108
  38.2 0.0 all-gather.5.cloned.1.call-done
  38.3 4.3 fusion.11
  42.6 52.4 %all-to-all-done.1 = bf16[32,1,16,4608]{3,2,1,0:T(8,128)(2,1)} async-done(((bf16[32,1,16,4608]{3,2,1,0:T(8,128)(2,1)}), bf16[32,1,16,4608]{3,2,1,0:T(8,128)(2,1)}, u32[]{:S(2)}, u32[]{:S(2)}) %all-to-all-start.1) | async-done | bytes 4718624 | tf_op jit(solution)/shard_map/all_to_all | solution.py:99
  95.0 3.0 gather_fusion
  98.0 0.0 copy-start.1
  98.0 0.7 multiply_reduce_fusion.1
  98.8 0.1 rsqrt.12
  98.9 113.5 %all-gather.3.cloned.1.call-done = bf16[4608,2048]{1,0:T(8,128)(2,1)} async-done(((bf16[1152,2048]{1,0:T(8,128)(2,1)}), bf16[4608,2048]{1,0:T(8,128)(2,1)}) %all-gather.3.cloned.1.call-update) | async-done | bytes 18874384 | tf_op jit(solution)/shard_map/all_gather | solution.py:44
  212.4 12.0 %multiply_reduce_fusion = (f32[256]{0:T(256)S(1)}, f32[256,4608]{1,0:T(8,128)}) fusion(f32[256]{0:T(256)S(1)} %rsqrt.12, bf16[16,16,4608]{2,1,0:T(8,128)(2,1)S(1)} %gather_fusion, pred[256]{0:T(512)(128)(4,1)S(1)} %broadcast_in_dim.108, f32[4608]{0:T(1024)S(1)} %convert_element_type.61, f32[256,4608]{1,0:T(8,128)} %fusion.11, ...), kind=kOutput, calls=%fused_computation.12 | convolution fusion | flops 4840095744 | bytes 31740160 | tf_op jit(solution)/shard_map/rq,dq->rd/dot_general | solution.py:58
  224.4 6.4 %multiply_convert_fusion = (bf16[256,4608]{1,0:T(8,128)(2,1)}, bf16[256,4608]{1,0:T(8,128)(2,1)S(1)}) fusion(f32[256,4608]{1,0:T(8,128)} %get-tuple-element.16, f32[256]{0:T(256)S(1)} %broadcast_multiply_fusion, f32[256]{0:T(256)S(1)} %rsqrt.12, bf16[16,16,4608]{2,1,0:T(8,128)(2,1)} %copy-done.1, pred[256]{0:T(512)(128)(4,1)S(1)} %broadcast_in_dim.108, ...), kind=kLoop, calls=%fused_computation.11 | loop fusion | flops 10616832 | bytes 11817216 | tf_op jit(solution)/shard_map/convert_element_type | solution.py:72
  230.8 4.7 %gather_fusion.1 = bf16[32,16,4608]{2,1,0:T(8,128)(2,1)} fusion(bf16[16,16,4608]{2,1,0:T(8,128)(2,1)} %bitcast.42, s32[1024]{0:T(1024)S(1)} %pad_clamp_fusion.1), kind=kCustom, calls=%fused_computation.3 | custom fusion | bytes 9437312 | tf_op jit(solution)/shard_map/jit(_take)/gather | solution.py:113
  235.5 5.1 %fusion.1 = bf16[32,1,16,4608]{3,2,1,0:T(8,128)(2,1)} fusion(bf16[32,16,4608]{2,1,0:T(8,128)(2,1)} %gather_fusion.1, pred[32]{0:T(512)(128)(4,1)S(1)} %compare_and_fusion.2, pred[32]{0:T(512)(128)(4,1)S(1)} %get-tuple-element.13), kind=kLoop, calls=%fused_computation.7 | loop fusion | flops 4718592 | bytes 9437248 | tf_op jit(solution)/shard_map/jit(_where)/select_n | solution.py:114
  240.6 7.6 %all-to-all-start.2 = ((bf16[32,1,16,4608]{3,2,1,0:T(8,128)(2,1)}), bf16[32,1,16,4608]{3,2,1,0:T(8,128)(2,1)}, u32[]{:S(2)}, u32[]{:S(2)}) async-start(bf16[32,1,16,4608]{3,2,1,0:T(8,128)(2,1)} %fusion.1), calls=%async_computation.2 | async-start | bytes 9437184 | tf_op jit(solution)/shard_map/all_to_all | solution.py:117
  248.2 0.2 all-reduce.3.cloned.1.call-start
  248.5 2.0 convolution_convert_fusion.1
  250.5 1.3 fusion.13
  251.8 2.2 fusion.12
  254.1 0.0 all-reduce.3.cloned.1.call-update
  254.1 1.5 fusion.10
  255.5 10.5 %fusion.3 = bf16[256,2048]{1,0:T(8,128)(2,1)} fusion(f32[256,2048]{1,0:T(8,128)S(1)} %fusion.10, bf16[256,4608]{1,0:T(8,128)(2,1)S(1)} %get-tuple-element.12, bf16[4608,2048]{1,0:T(8,128)(2,1)} %all-gather.3.cloned.1.call-done), kind=kOutput, calls=%fused_computation.17 | convolution fusion | flops 4832886784 | bytes 24379392 | tf_op jit(solution)/shard_map/dot_general | solution.py:47
  266.0 44.1 %all-to-all-done.2 = bf16[32,1,16,4608]{3,2,1,0:T(8,128)(2,1)} async-done(((bf16[32,1,16,4608]{3,2,1,0:T(8,128)(2,1)}), bf16[32,1,16,4608]{3,2,1,0:T(8,128)(2,1)}, u32[]{:S(2)}, u32[]{:S(2)}) %all-to-all-start.2) | async-done | bytes 4718624 | tf_op jit(solution)/shard_map/all_to_all | solution.py:117
  310.2 5.4 %gather_fusion.3 = bf16[32,16,4608]{2,1,0:T(8,128)(2,1)} fusion(bf16[32,16,4608]{2,1,0:T(8,128)(2,1)} %bitcast.10, s32[1024]{0:T(1024)S(1)} %pad_clamp_fusion), kind=kCustom, calls=%fused_computation.1.clone | custom fusion | bytes 9437312 | tf_op jit(solution)/shard_map/jit(_take)/gather | solution.py:118
  315.6 5.2 %select_select_fusion = bf16[32,16,4608]{2,1,0:T(8,128)(2,1)} fusion(bf16[32,16,4608]{2,1,0:T(8,128)(2,1)} %gather_fusion.3, pred[32]{0:T(512)(128)(4,1)S(1)} %get-tuple-element.9, pred[32]{0:T(512)(128)(4,1)S(1)} %broadcast_compare_fusion), kind=kLoop, calls=%fused_computation.8 | loop fusion | flops 4718592 | bytes 9437248 | tf_op jit(solution)/shard_map/jit(_where)/select_n | solution.py:121
  320.8 116.6 %all-reduce.3.cloned.1.call-done = (f32[4608,128]{1,0:T(8,128)}, f32[128,2048]{1,0:T(8,128)}) async-done(((f32[4608,128]{1,0:T(8,128)}, f32[128,2048]{1,0:T(8,128)}), (f32[4608,128]{1,0:T(8,128)}, f32[128,2048]{1,0:T(8,128)})) %all-reduce.3.cloned.1.call-update) | async-done | bytes 3407888 | tf_op jit(solution)/shard_map/psum | solution.py:124
  437.4 3.3 copy.22
  440.7 1.0 copy.23
  (27 shorter events, 0.1 us)
Async XLA Ops:
  7.2 29.4 %copy-start = (bf16[256,2048]{1,0:T(8,128)(2,1)S(1)}, bf16[256,2048]{1,0:T(8,128)(2,1)}, u32[]{:S(2)}) copy-start(bf16[256,2048]{1,0:T(8,128)(2,1)} %param.17) | copy-start | bytes 3145732
  7.2 1.5 copy-start.6
  7.2 1.5 copy-start.5
  7.2 31.1 %all-gather.5.cloned.1.call-start = ((), (), s32[]{:S(2)}) async-start(), calls=%async_computation.4 | async-start | bytes 1474560 | tf_op jit(solution)/shard_map/all_gather | solution.py:45
  7.9 204.4 %all-gather.3.cloned.1.call-start = ((), (), s32[]{:S(2)}) async-start(), calls=%async_computation.3 | async-start | bytes 23592960 | tf_op jit(solution)/shard_map/all_gather | solution.py:44
  9.8 19.2 %all-to-all-start = ((bf16[32,1,1]{2,1,0:T(2,128)(2,1)}), bf16[32,1,1]{2,1,0:T(2,128)(2,1)S(1)}, u32[]{:S(2)}, u32[]{:S(2)}) async-start(bf16[32,1,1]{2,1,0:T(2,128)(2,1)} %copy.18), calls=%async_computation | async-start | bytes 32768 | tf_op jit(solution)/shard_map/all_to_all | solution.py:100
  29.0 7.6 %copy-start.4 = (bf16[4608]{0:T(1024)(128)(2,1)S(1)}, bf16[4608]{0:T(1024)(128)(2,1)}, u32[]{:S(2)}) copy-start(bf16[4608]{0:T(1024)(128)(2,1)} %param.11) | copy-start | bytes 27652
  29.0 7.6 %copy-start.2 = (bf16[128,2048]{1,0:T(8,128)(2,1)S(1)}, bf16[128,2048]{1,0:T(8,128)(2,1)}, u32[]{:S(2)}) copy-start(bf16[128,2048]{1,0:T(8,128)(2,1)} %param.14) | copy-start | bytes 1572868
  29.0 66.0 %all-to-all-start.1 = ((bf16[32,1,16,4608]{3,2,1,0:T(8,128)(2,1)}), bf16[32,1,16,4608]{3,2,1,0:T(8,128)(2,1)}, u32[]{:S(2)}, u32[]{:S(2)}) async-start(bf16[32,1,16,4608]{3,2,1,0:T(8,128)(2,1)} %fusion.2), calls=%async_computation.1 | async-start | bytes 9437184 | tf_op jit(solution)/shard_map/all_to_all | solution.py:99
  98.0 126.4 %copy-start.1 = (bf16[16,16,4608]{2,1,0:T(8,128)(2,1)}, bf16[16,16,4608]{2,1,0:T(8,128)(2,1)S(1)}, u32[]{:S(2)}) copy-start(bf16[16,16,4608]{2,1,0:T(8,128)(2,1)S(1)} %gather_fusion) | copy-start | bytes 7077892
  240.6 69.6 %all-to-all-start.2 = ((bf16[32,1,16,4608]{3,2,1,0:T(8,128)(2,1)}), bf16[32,1,16,4608]{3,2,1,0:T(8,128)(2,1)}, u32[]{:S(2)}, u32[]{:S(2)}) async-start(bf16[32,1,16,4608]{3,2,1,0:T(8,128)(2,1)} %fusion.1), calls=%async_computation.2 | async-start | bytes 9437184 | tf_op jit(solution)/shard_map/all_to_all | solution.py:117
  248.2 189.1 %all-reduce.3.cloned.1.call-start = ((), (), s32[]{:S(2)}) async-start(), calls=%async_computation.5 | async-start | bytes 6815744 | tf_op jit(solution)/shard_map/psum | solution.py:124
  437.4 3.3 copy-start.3
Sparse Core Ops, SparseCore 0:
  9.7 26.8 all-gather.4
  38.3 174.0 all-gather.2
  254.7 182.6 all-reduce.2
where the time goes:
time: 449 us; the launch traced here: 448 us
  waiting for transfers between devices  328 us (73%)
  matrix products  34.3 us (8%)
  other arithmetic  24.1 us (5%)
  starting transfers between devices  24 us (5%)
  local copies, waits for them, and re-layouts  23.8 us (5%)
  between operations  14 us (3%)
    psum x1, waiting for transfers between devices, body(): grad_down, grad_up = lax.psum((grad_down, grad_up), ('dp', 'fsdp'))  117 us
    all_gather x1, waiting for transfers between devices, project_surviving(): lax.all_gather(tied_query_matrix, 'fsdp', axis=0, tiled=True)  113 us
    all_to_all x1, waiting for transfers between devices, body(): lax.all_to_all(send_rows, 'dp', split_axis=0, concat_axis=0, tiled=True)  52.4 us
    all_to_all x1, waiting for transfers between devices, body(): lax.all_to_all(back, 'dp', split_axis=0, concat_axis=0, tiled=True)  44.1 us
    dot_general x1, matrix products, project_surviving(): jnp.einsum('rq,dq->rd', incoming_gradient_rows, full_weight, preferred_el...  12 us
    dot_general x1, matrix products, project_surviving(): jnp.dot(normalized_blocks, full_weight, preferred_element_type=jnp.float32)  10.5 us
  transfers between devices with their start and end apart: 6, of which 4 were waited for; matrix products, arithmetic and copies ran while one was open for 11% of the time, Pallas kernels for 0%

commit v1 on v0

--- a/solution.py
+++ b/solution.py
@@ -2,6 +2,7 @@
 import jax.numpy as jnp
 from jax import lax
 from jax.sharding import PartitionSpec as P
+from jax.lax import all_to_all, axis_size
 
 
 def arrange(live, target, dp_count, slot_count):
@@ -41,7 +42,9 @@
     gain_f = rmsnorm_gain_vector.astype(jnp.float32)
     normalized_blocks = (normed * gain_f).astype(jnp.bfloat16)
     full_weight, full_down = (
-        lax.all_gather(tied_query_matrix, "fsdp", axis=0, tiled=True),
+        jnp.concatenate(
+            all_to_all(jnp.stack([tied_query_matrix] * axis_size("fsdp")), "fsdp", 0, 0), axis=0
+        ),
         lax.all_gather(adapter_down_matrix, "fsdp", axis=0, tiled=True),
     )
     shared_output = jnp.dot(normalized_blocks, full_weight, preferred_element_type=jnp.float32)

time: 449 us -> 556 us (1.24)
  blocking collectives: 0 us -> 64.3 us
  waiting for transfers between devices: 328 us -> 365 us
    all_to_all x1, waiting for transfers between devices: 52.4 us -> 175 us  [project_surviving(): all_to_all(jnp.stack([tied_query_matrix] * axis_size('fsdp')), 'fsdp', 0, 0)]
    all_gather x1 -> x0, waiting for transfers between devices: 113 us -> none  [project_surviving(): lax.all_gather(tied_query_matrix, 'fsdp', axis=0, tiled=True)]
    all_to_all x0 -> x1, blocking collectives: none -> 64.3 us  [body(): lax.all_to_all(send_rows, 'dp', split_axis=0, concat_axis=0, tiled=True)]
    all_gather x1, waiting for transfers between devices: 0.02 us -> 31.7 us  [project_surviving(): lax.all_gather(adapter_down_matrix, 'fsdp', axis=0, tiled=True)]
    another operation x0 -> x1, local copies, waits for them, and re-layouts: none -> 6.84 us  [project_surviving(): jnp.stack([tied_query_matrix] * axis_size('fsdp'))]
  transfers between devices with their start and end apart: 6 -> 5, of which waited for: 4 -> 4; matrix products, arithmetic and copies ran while one was open for 11% -> 9% of each run, Pallas kernels for 0% -> 0%
where the time goes in v1:
time: 556 us; the launch traced here: 555 us
  waiting for transfers between devices  365 us (66%)
  blocking collectives  64.3 us (12%)
  matrix products  34.1 us (6%)
  local copies, waits for them, and re-layouts  29.1 us (5%)
  other arithmetic  26.4 us (5%)
  starting transfers between devices  21.3 us (4%)
  between operations  14.3 us (3%)
    all_to_all x1, waiting for transfers between devices, project_surviving(): all_to_all(jnp.stack([tied_query_matrix] * axis_size('fsdp')), 'fsdp', 0, 0)  175 us
    psum x1, waiting for transfers between devices, body(): grad_down, grad_up = lax.psum((grad_down, grad_up), ('dp', 'fsdp'))  116 us
    all_to_all x1, blocking collectives, body(): lax.all_to_all(send_rows, 'dp', split_axis=0, concat_axis=0, tiled=True)  64.3 us
    all_to_all x1, waiting for transfers between devices, body(): lax.all_to_all(back, 'dp', split_axis=0, concat_axis=0, tiled=True)  42.2 us
    all_gather x1, waiting for transfers between devices, project_surviving(): lax.all_gather(adapter_down_matrix, 'fsdp', axis=0, tiled=True)  31.7 us
    dot_general x1, matrix products, project_surviving(): jnp.einsum('rq,dq->rd', incoming_gradient_rows, full_weight, preferred_el...  12.4 us
  transfers between devices with their start and end apart: 5, of which 4 were waited for; matrix products, arithmetic and copies ran while one was open for 9% of the time, Pallas kernels for 0%

profile of v1, /device:TPU:1, one launch (start us, length us, event | category | flops | bytes accessed | tf_op | source)
XLA Modules:
  0.0 554.9 jit_solution(6331547685246185587)
XLA Ops:
  7.2 0.0 copy-start
  7.2 0.7 broadcast_compare_fusion
  7.9 0.9 convert_reduce_fusion
  8.8 0.7 compare_and_fusion
  9.5 0.1 fusion.11
  9.6 0.7 copy.18
  10.4 8.6 %all-to-all-start = ((bf16[32,1,1]{2,1,0:T(2,128)(2,1)}), bf16[32,1,1]{2,1,0:T(2,128)(2,1)S(1)}, u32[]{:S(2)}, u32[]{:S(2)}) async-start(bf16[32,1,1]{2,1,0:T(2,128)(2,1)} %copy.18), calls=%async_computation | async-start | bytes 32768 | tf_op jit(solution)/shard_map/all_to_all | solution.py:103
  18.9 0.1 select_reduce_fusion
  19.1 5.4 gather_fusion.2
  24.5 5.1 fusion.5
  29.6 64.3 %all_to_all.21 = bf16[32,1,16,4608]{3,2,1,0:T(8,128)(2,1)} all-to-all(bf16[32,1,16,4608]{3,2,1,0:T(8,128)(2,1)} %fusion.5), channel_id=1, replica_groups=mesh['dp'=32,'fsdp'=4] {'dp'}, dimensions={0} | all-to-all | bytes 9437184 | tf_op jit(solution)/shard_map/all_to_all | solution.py:102
  93.9 6.8 %stack.2 = bf16[4,1152,2048]{2,1,0:T(8,128)(2,1)} broadcast(bf16[1152,2048]{1,0:T(8,128)(2,1)S(1)} %copy-done.4), dimensions={1,2} | broadcast | bytes 23592960 | tf_op jit(solution)/shard_map/stack | solution.py:46
  100.7 7.5 %all-to-all-start.2 = ((bf16[4,1152,2048]{2,1,0:T(8,128)(2,1)}), bf16[4,1152,2048]{2,1,0:T(8,128)(2,1)}, u32[]{:S(2)}, u32[]{:S(2)}) async-start(bf16[4,1152,2048]{2,1,0:T(8,128)(2,1)} %stack.2), calls=%async_computation.2 | async-start | bytes 37748736 | tf_op jit(solution)/shard_map/all_to_all | solution.py:46
  108.2 0.0 all-gather.2.cloned.1.call-start
  108.3 0.7 all-gather.2.cloned.1.call-update
  109.0 0.4 convolution_convert_fusion
  109.4 0.7 compare_reduce_fusion
  110.1 0.1 reduce-window.4
  110.2 0.1 fusion.8
  110.3 0.1 select_reduce_fusion.1
  110.4 0.1 broadcast_in_dim.112
  110.5 0.1 broadcast_in_dim.113
  110.6 31.7 %all-gather.2.cloned.1.call-done = bf16[4608,128]{1,0:T(8,128)(2,1)} async-done(((bf16[1152,128]{1,0:T(8,128)(2,1)}), bf16[4608,128]{1,0:T(8,128)(2,1)}) %all-gather.2.cloned.1.call-update) | async-done | bytes 1179664 | tf_op jit(solution)/shard_map/all_gather | solution.py:48
  142.3 4.2 fusion.15
  146.6 3.0 gather_fusion
  149.6 0.7 fusion.1
  150.4 0.1 rsqrt.13
  150.5 174.6 %all-to-all-done.2 = bf16[4,1152,2048]{2,1,0:T(8,128)(2,1)} async-done(((bf16[4,1152,2048]{2,1,0:T(8,128)(2,1)}), bf16[4,1152,2048]{2,1,0:T(8,128)(2,1)}, u32[]{:S(2)}, u32[]{:S(2)}) %all-to-all-start.2) | async-done | bytes 18874400 | tf_op jit(solution)/shard_map/all_to_all | solution.py:46
  325.0 12.4 %multiply_reduce_fusion = (f32[256]{0:T(256)S(1)}, bf16[256,4608]{1,0:T(8,128)(2,1)}, f32[256,4608]{1,0:T(8,128)}) fusion(f32[256]{0:T(256)S(1)} %rsqrt.13, bf16[16,16,4608]{2,1,0:T(8,128)(2,1)S(1)} %gather_fusion, pred[256]{0:T(512)(128)(4,1)S(1)} %broadcast_in_dim.113, f32[4608]{0:T(1024)S(1)} %convert_element_type.78, f32[256,4608]{1,0:T(8,128)} %fusion.15, ...), kind=kOutput, calls=%fused_computation.17 | convolution fusion | flops 4840095744 | bytes 34099456 | tf_op jit(solution)/shard_map/rq,dq->rd/dot_general | solution.py:61
  337.4 4.3 multiply_convert_fusion
  341.7 3.0 gather_fusion.1
  344.8 5.1 fusion.4
  349.9 5.0 all-to-all-start.3
  354.9 0.2 all-reduce.3.cloned.1.call-start
  355.2 2.3 fusion.3
  357.5 0.9 convolution_convert_fusion.1
  358.5 1.3 fusion.16
  359.8 2.4 fusion.7
  362.2 0.0 all-reduce.3.cloned.1.call-update
  362.2 1.6 fusion.14
  363.9 0.2 copy-done.5
  364.1 10.8 %fusion.6 = bf16[256,2048]{1,0:T(8,128)(2,1)} fusion(f32[256,2048]{1,0:T(8,128)S(1)} %fusion.14, bf16[256,4608]{1,0:T(8,128)(2,1)S(1)} %bitcast.41, bf16[4608,2048]{1,0:T(8,128)(2,1)} %bitcast.8), kind=kOutput, calls=%fused_computation.21 | convolution fusion | flops 4832886784 | bytes 24379392 | tf_op jit(solution)/shard_map/dot_general | solution.py:50
  374.8 42.2 %all-to-all-done.3 = bf16[32,1,16,4608]{3,2,1,0:T(8,128)(2,1)} async-done(((bf16[32,1,16,4608]{3,2,1,0:T(8,128)(2,1)}), bf16[32,1,16,4608]{3,2,1,0:T(8,128)(2,1)}, u32[]{:S(2)}, u32[]{:S(2)}) %all-to-all-start.3) | async-done | bytes 4718624 | tf_op jit(solution)/shard_map/all_to_all | solution.py:120
  417.0 5.4 gather_fusion.3
  422.4 5.2 select_select_fusion
  427.6 116.2 %all-reduce.3.cloned.1.call-done = (f32[4608,128]{1,0:T(8,128)}, f32[128,2048]{1,0:T(8,128)}) async-done(((f32[4608,128]{1,0:T(8,128)}, f32[128,2048]{1,0:T(8,128)}), (f32[4608,128]{1,0:T(8,128)}, f32[128,2048]{1,0:T(8,128)})) %all-reduce.3.cloned.1.call-update) | async-done | bytes 3407888 | tf_op jit(solution)/shard_map/psum | solution.py:127
  543.8 3.3 copy.22
  547.1 1.0 copy.23
  (35 shorter events, 0.1 us)
Async XLA Ops:
  7.2 101.8 %copy-start = (bf16[256,2048]{1,0:T(8,128)(2,1)S(1)}, bf16[256,2048]{1,0:T(8,128)(2,1)}, u32[]{:S(2)}) copy-start(bf16[256,2048]{1,0:T(8,128)(2,1)} %param.17) | copy-start | bytes 3145732
  10.4 19.2 %all-to-all-start = ((bf16[32,1,1]{2,1,0:T(2,128)(2,1)}), bf16[32,1,1]{2,1,0:T(2,128)(2,1)S(1)}, u32[]{:S(2)}, u32[]{:S(2)}) async-start(bf16[32,1,1]{2,1,0:T(2,128)(2,1)} %copy.18), calls=%async_computation | async-start | bytes 32768 | tf_op jit(solution)/shard_map/all_to_all | solution.py:103
  29.6 64.3 %copy-start.4 = (bf16[1152,2048]{1,0:T(8,128)(2,1)S(1)}, bf16[1152,2048]{1,0:T(8,128)(2,1)}, u32[]{:S(2)}) copy-start(bf16[1152,2048]{1,0:T(8,128)(2,1)} %param.12) | copy-start | bytes 14155780
  100.7 8.2 %copy-start.10 = (bf16[4608]{0:T(1024)(128)(2,1)S(1)}, bf16[4608]{0:T(1024)(128)(2,1)}, u32[]{:S(2)}) copy-start(bf16[4608]{0:T(1024)(128)(2,1)} %param.11) | copy-start | bytes 27652
  100.7 8.3 %copy-start.6 = (bf16[128,2048]{1,0:T(8,128)(2,1)S(1)}, bf16[128,2048]{1,0:T(8,128)(2,1)}, u32[]{:S(2)}) copy-start(bf16[128,2048]{1,0:T(8,128)(2,1)} %param.14) | copy-start | bytes 1572868
  100.7 224.3 %all-to-all-start.2 = ((bf16[4,1152,2048]{2,1,0:T(8,128)(2,1)}), bf16[4,1152,2048]{2,1,0:T(8,128)(2,1)}, u32[]{:S(2)}, u32[]{:S(2)}) async-start(bf16[4,1152,2048]{2,1,0:T(8,128)(2,1)} %stack.2), calls=%async_computation.2 | async-start | bytes 37748736 | tf_op jit(solution)/shard_map/all_to_all | solution.py:46
  108.2 34.1 %all-gather.2.cloned.1.call-start = ((), (), s32[]{:S(2)}) async-start(), calls=%async_computation.4 | async-start | bytes 1474560 | tf_op jit(solution)/shard_map/all_gather | solution.py:48
  149.6 187.8 %copy-start.1 = (bf16[16,16,4608]{2,1,0:T(8,128)(2,1)}, bf16[16,16,4608]{2,1,0:T(8,128)(2,1)S(1)}, u32[]{:S(2)}) copy-start(bf16[16,16,4608]{2,1,0:T(8,128)(2,1)S(1)} %gather_fusion) | copy-start | bytes 7077892
  349.9 5.3 copy-start.2
  349.9 67.1 %all-to-all-start.3 = ((bf16[32,1,16,4608]{3,2,1,0:T(8,128)(2,1)}), bf16[32,1,16,4608]{3,2,1,0:T(8,128)(2,1)}, u32[]{:S(2)}, u32[]{:S(2)}) async-start(bf16[32,1,16,4608]{3,2,1,0:T(8,128)(2,1)} %fusion.4), calls=%async_computation.3 | async-start | bytes 9437184 | tf_op jit(solution)/shard_map/all_to_all | solution.py:120
  354.9 188.9 %all-reduce.3.cloned.1.call-start = ((), (), s32[]{:S(2)}) async-start(), calls=%async_computation.5 | async-start | bytes 6815744 | tf_op jit(solution)/shard_map/psum | solution.py:127
  355.1 2.4 copy-start.3
  355.1 2.4 copy-start.7
  358.4 1.3 copy-start.9
  362.2 1.9 copy-start.5
  543.8 3.3 copy-start.8
Sparse Core Ops, SparseCore 0:
  110.7 31.5 all-gather.1
  362.4 181.3 all-reduce.2
